TPU v7x, 32 devices: a whole 2x2x4 slice. The times are simulated.
32 devices in a mesh: parts: 2 (over y), row: 4 (over z), col: 4 (over x, core).
Axes of the slice: x: 2, y: 2, z: 4, core: 2. Of those that a mesh axis runs over, the one named last changes fastest.
Arguments:
- pair: bfloat16 [384, 192, 128], P(('parts', 'row'), 'col'), parts along dimension 0, may hold values from -6 to 6
- mask: int32 [384], P('parts'), parts along dimension 0, may hold values 0 or 1
- in_weights: bfloat16 [128, 512], replicated, may hold values from -0.5 to 0.5
- gate_weight: bfloat16 [128, 128], replicated, may hold values from -0.5 to 0.5
- out_weight: bfloat16 [128, 128], replicated, may hold values from -0.5 to 0.5
Outputs:
- update: bfloat16 [384, 192, 128], P(('parts', 'row'), 'col'), parts along dimension 0
There are 2 independent parts, one for each index of `parts`. A program takes and returns all parts, laid end to end along the dimension named above; an argument that names none is the same for every part. Nothing has to cross between parts.
Inputs may be any that keep to these rules, and one draw needn't show every extreme that they name: `mask`: 1 for a real residue, 0 for padding.
All inputs are finite; a program needn't handle non-finite values.
Results may differ from a plain program's by a relative error of at most 0.008.
Values may be sent and summed in bfloat16 or wider, within the bound.
A program may use at most 128 MiB of HBM per device.

v0:
```python
import jax
import jax.numpy as jnp
from jax import lax
from jax.sharding import PartitionSpec as P


def normalize(values):
    values = values.astype(jnp.float32)
    mean = jnp.mean(values, axis=-1, keepdims=True)
    centered = values - mean
    var = jnp.mean(centered * centered, axis=-1, keepdims=True)
    return centered * lax.rsqrt(var + 1e-05)


def project(block, weights):
    flat = block.reshape(-1, block.shape[-1])
    result = jnp.dot(flat, weights, preferred_element_type=jnp.float32)
    return result.reshape(block.shape[0], block.shape[1], weights.shape[1])


def gated(proj, first_flags, second_flags, hidden):
    both = first_flags[:, None, None] * second_flags[None, :, None]
    return (jax.nn.sigmoid(proj[..., :hidden]) * proj[..., hidden:] * both).astype(jnp.bfloat16)


def per_device(pair, mask, in_weights, gate_weight, out_weight):
    rows, cols, width = pair.shape
    hidden = out_weight.shape[0]
    parts = lax.axis_size("col")
    step = rows // parts
    total = mask.shape[0]
    groups = total // rows
    row_at = lax.axis_index("row")
    col_at = lax.axis_index("col")
    flags = mask.astype(jnp.float32)
    row_flags = lax.dynamic_slice_in_dim(flags, row_at * rows, rows)
    col_flags = lax.dynamic_slice_in_dim(flags, col_at * cols, cols)
    normed = normalize(pair).astype(jnp.bfloat16)
    right_own = gated(project(normed, in_weights[:, 2 * hidden :]), row_flags, col_flags, hidden)
    mirrored = lax.all_to_all(
        lax.all_to_all(normed, "col", split_axis=0, concat_axis=1, tiled=True),
        "row",
        split_axis=1,
        concat_axis=0,
        tiled=True,
    )
    spread = flags.reshape(groups, parts, step)
    mirror_flags = lax.dynamic_index_in_dim(spread, col_at, 1, False).reshape(-1)
    left = gated(project(mirrored, in_weights[:, : 2 * hidden]), mirror_flags, row_flags, hidden)
    right = lax.all_gather(right_own, "row", axis=0, tiled=True)
    right_split = right.reshape(groups, parts, step, cols, hidden)
    span = groups * step
    piece = lax.all_gather(left, "col", axis=0, tiled=True)
    count = piece.shape[0] // span
    pieces = piece.reshape(count, groups, step, piece.shape[1], hidden)
    mixed = jnp.einsum("nqtic,qntjc->ijc", pieces, right_split, preferred_element_type=jnp.float32)
    mixed_normed = normalize(mixed).astype(jnp.bfloat16)
    gate = jax.nn.sigmoid(project(normed, gate_weight))
    value = project(mixed_normed, out_weight)
    return (gate * value).astype(jnp.bfloat16)


def solution(mesh):
    placed = (P(("parts", "row"), "col", None), P("parts"), P(), P(), P())
    return jax.shard_map(
        per_device,
        mesh=mesh,
        in_specs=placed,
        out_specs=P(("parts", "row"), "col", None),
        check_vma=False,
    )
```

profile of v0, /device:TPU:17, one launch (start us, length us, event | category | flops | bytes accessed | tf_op | source)
XLA Modules:
  0.0 140.6 jit_solution(3335886447278498385)
XLA Ops:
  6.5 0.0 copy-start
  6.5 0.0 copy-start.1
  6.5 0.0 all-gather.3.cloned.1.call-start
  6.5 0.7 convert_element_type.23
  7.3 0.1 reshape.119
  7.4 0.1 mul.103
  7.5 0.0 copy-start.3
  7.5 1.5 %convert_reduce_fusion = f32[48,48]{1,0:T(8,128)S(1)} fusion(bf16[48,48,128]{2,1,0:T(8,128)(2,1)} %param.5), kind=kLoop, calls=%fused_computation.5 | loop fusion | flops 587520 | bytes 599040 | tf_op jit(solution)/shard_map/reduce_sum | solution.py:9
  9.0 1.8 %fusion.6 = f32[48,48]{1,0:T(8,128)S(1)} fusion(bf16[48,48,128]{2,1,0:T(8,128)(2,1)} %param.5, f32[48,48]{1,0:T(8,128)S(1)} %broadcast_multiply_fusion.3), kind=kLoop, calls=%fused_computation.14 | loop fusion | flops 1177344 | bytes 608256 | tf_op jit(solution)/shard_map/reduce_sum | solution.py:11
  10.8 0.0 copy-done.1
  10.8 0.8 fusion.7
  11.6 0.1 fusion.26
  11.7 0.0 copy-done.3
  11.7 0.4 fusion.20
  12.1 0.1 broadcast_multiply_fusion
  12.2 1.2 fusion.14
  13.4 0.0 all-gather.3.cloned.1.call-update
  13.4 0.0 all-gather.5.cloned.1.call-start
  13.5 12.3 %all_to_all.33 = bf16[48,48,128]{2,1,0:T(8,128)(2,1)S(1)} all-to-all(bf16[48,48,128]{2,1,0:T(8,128)(2,1)S(1)} %fusion.7), channel_id=1, replica_groups=mesh['parts'=2,'row'=4,'col'=4] {'col'}, dimensions={0} | all-to-all | bytes 1179648 | tf_op jit(solution)/shard_map/all_to_all | solution.py:41
  25.8 0.1 copy.41
  25.9 0.4 copy.42
  26.3 42.5 %all_to_all.34 = bf16[12,192,128]{2,0,1:T(8,128)(2,1)S(1)} all-to-all(bf16[12,192,128]{2,0,1:T(8,128)(2,1)S(1)} %copy.42), channel_id=1, replica_groups=mesh['parts'=2,'row'=4,'col'=4] {'row'}, dimensions={1} | all-to-all | bytes 1179648 | tf_op jit(solution)/shard_map/all_to_all | solution.py:40
  68.8 0.2 copy.44
  68.9 0.4 fusion.18
  69.4 1.2 fusion.9
  70.6 0.0 all-gather.5.cloned.1.call-update
  70.6 0.0 copy-done
  70.6 1.5 %fusion.4 = f32[48,48,128]{2,1,0:T(8,128)} fusion(bf16[48,48,128]{2,1,0:T(8,128)(2,1)S(1)} %fusion.7, bf16[128,128]{1,0:T(8,128)(2,1)S(1)} %copy-done), kind=kOutput, calls=%fused_computation.12 | convolution fusion | flops 76382208 | bytes 1802240 | tf_op jit(solution)/shard_map/dot_general | solution.py:17
  72.1 6.4 %all-gather.3.cloned.1.call-done = bf16[192,48,128]{2,1,0:T(8,128)(2,1)} async-done(((bf16[48,48,128]{2,1,0:T(8,128)(2,1)}), bf16[192,48,128]{2,1,0:T(8,128)(2,1)}) %all-gather.3.cloned.1.call-update) | async-done | bytes 2359312 | tf_op jit(solution)/shard_map/all_gather | solution.py:50
  78.5 12.9 %copy.45 = bf16[4,4,12,48,128]{3,2,0,1,4:T(8,128)(2,1)} copy(bf16[4,4,12,48,128]{4,3,2,1,0:T(8,128)(2,1)} %bitcast.42) | data formatting | bytes 4718592 | tf_op jit(solution)/shard_map/reshape | solution.py:51
  91.4 14.9 %all-gather.5.cloned.1.call-done = bf16[192,48,128]{2,1,0:T(8,128)(2,1)} async-done(((bf16[48,48,128]{2,1,0:T(8,128)(2,1)}), bf16[192,48,128]{2,1,0:T(8,128)(2,1)}) %all-gather.5.cloned.1.call-update) | async-done | bytes 2359312 | tf_op jit(solution)/shard_map/all_gather | solution.py:53
  106.4 12.8 %copy.46 = bf16[4,4,12,48,128]{3,2,1,0,4:T(8,128)(2,1)} copy(bf16[4,4,12,48,128]{4,3,2,1,0:T(8,128)(2,1)} %bitcast.43) | data formatting | bytes 4718592 | tf_op jit(solution)/shard_map/reshape | solution.py:55
  119.2 8.7 %bitcast_reduce_fusion = (f32[48,48]{0,1:T(8,128)S(1)}, f32[128,48,48,1,1]{2,1,4,3,0:T(8,128)S(1)}) fusion(bf16[4,4,12,48,128]{3,2,0,1,4:T(8,128)(2,1)} %copy.45, bf16[4,4,12,48,128]{3,2,1,0,4:T(8,128)(2,1)} %copy.46), kind=kOutput, calls=%fused_computation.1 | convolution fusion | flops 113538816 | bytes 5907456 | tf_op jit(solution)/shard_map/nqtic,qntjc->ijc/dot_general | solution.py:56
  127.9 0.1 copy.47
  128.0 0.1 copy.48
  128.1 0.5 multiply_reduce_fusion
  128.6 0.1 copy.49
  128.7 0.1 copy.50
  128.7 1.5 %multiply_convert_fusion = bf16[48,48,128]{0,1,2:T(8,128)(2,1)} fusion(f32[128,48,48,1,1]{2,1,4,3,0:T(8,128)S(1)} %get-tuple-element.10, f32[48,48]{0,1:T(8,128)S(1)} %copy.50, f32[48,48]{0,1:T(8,128)S(1)} %copy.48), kind=kLoop, calls=%fused_computation.2 | loop fusion | flops 884736 | bytes 1787904 | tf_op jit(solution)/shard_map/convert_element_type | solution.py:57
  130.3 0.0 copy-start.2
  130.3 0.0 copy-start.4
  130.3 2.4 %copy.51 = bf16[48,48,128]{2,1,0:T(8,128)(2,1)S(1)} copy(bf16[48,48,128]{0,1,2:T(8,128)(2,1)} %multiply_convert_fusion) | data formatting | bytes 1179648 | tf_op jit(solution)/shard_map/convert_element_type | solution.py:57
  132.6 0.0 copy-done.2
  132.6 0.0 copy-done.4
  132.6 1.1 fusion.5
  (5 shorter events, 0.1 us)
Async XLA Ops:
  6.5 64.1 %copy-start = (bf16[128,128]{1,0:T(8,128)(2,1)S(1)}, bf16[128,128]{1,0:T(8,128)(2,1)}, u32[]{:S(2)}) copy-start(bf16[128,128]{1,0:T(8,128)(2,1)} %param.8) | copy-start | bytes 98308
  6.5 4.2 %copy-start.1 = (bf16[48,48,128]{2,1,0:T(8,128)(2,1)S(1)}, bf16[48,48,128]{2,1,0:T(8,128)(2,1)}, u32[]{:S(2)}) copy-start(bf16[48,48,128]{2,1,0:T(8,128)(2,1)} %param.5) | copy-start | bytes 1769476
  6.5 72.0 %all-gather.3.cloned.1.call-start = ((), (), s32[]{:S(2)}) async-start(), calls=%async_computation.2 | async-start | bytes 2949120 | tf_op jit(solution)/shard_map/all_gather | solution.py:50
  7.5 4.2 %copy-start.3 = (bf16[128,512]{1,0:T(8,128)(2,1)S(1)}, bf16[128,512]{1,0:T(8,128)(2,1)}, u32[]{:S(2)}) copy-start(bf16[128,512]{1,0:T(8,128)(2,1)} %param.7) | copy-start | bytes 393220
  13.4 92.9 %all-gather.5.cloned.1.call-start = ((), (), s32[]{:S(2)}) async-start(), calls=%async_computation.3 | async-start | bytes 2949120 | tf_op jit(solution)/shard_map/all_gather | solution.py:53
  130.3 2.4 %copy-start.2 = (f32[48,48,128]{2,1,0:T(8,128)S(1)}, f32[48,48,128]{2,1,0:T(8,128)}, u32[]{:S(2)}) copy-start(f32[48,48,128]{2,1,0:T(8,128)} %fusion.4) | copy-start | bytes 3538948
  130.3 2.4 %copy-start.4 = (bf16[128,128]{1,0:T(8,128)(2,1)S(1)}, bf16[128,128]{1,0:T(8,128)(2,1)}, u32[]{:S(2)}) copy-start(bf16[128,128]{1,0:T(8,128)(2,1)} %param.9) | copy-start | bytes 98308
Sparse Core Ops, SparseCore 0:
  13.6 64.9 all-gather.2
  80.1 26.2 all-gather.4
where the time goes:
time: 142 us; the launch traced here: 141 us
  blocking collectives  54.8 us (39%)
  local copies, waits for them, and re-layouts  29.3 us (21%)
  waiting for transfers between devices  21.4 us (15%)
  between operations  13.5 us (10%)
  matrix products  12.2 us (9%)
  other arithmetic  9.3 us (7%)
    all_to_all x1, blocking collectives, per_device(): lax.all_to_all(lax.all_to_all(normed, 'col', split_axis=0, concat_axis=1,...  42.5 us
    all_gather x1, waiting for transfers between devices, per_device(): piece = lax.all_gather(left, 'col', axis=0, tiled=True)  14.9 us
    reshape x1, local copies, waits for them, and re-layouts, per_device(): right_split = right.reshape(groups, parts, step, cols, hidden)  12.9 us
    reshape x1, local copies, waits for them, and re-layouts, per_device(): pieces = piece.reshape(count, groups, step, piece.shape[1], hidden)  12.8 us
    all_to_all x1, blocking collectives, per_device(): lax.all_to_all(normed, 'col', split_axis=0, concat_axis=1, tiled=True)  12.3 us
    dot_general x1, matrix products, per_device(): jnp.einsum('nqtic,qntjc->ijc', pieces, right_split, preferred_element_typ...  8.75 us
    all_gather x1, waiting for transfers between devices, per_device(): right = lax.all_gather(right_own, 'row', axis=0, tiled=True)  6.45 us
    dot_general x4, matrix products, project(): result = jnp.dot(flat, weights, preferred_element_type=jnp.float32)  3.49 us
  transfers between devices with their start and end apart: 2, of which 2 were waited for; matrix products, arithmetic and copies ran while one was open for 12% of the time, Pallas kernels for 0%

commit v1 on v0

v1 whole, which is shorter than its diff:
```python
import jax
import jax.numpy as jnp
from jax import lax
from jax.sharding import PartitionSpec as P


def normalize(values):
    values = values.astype(jnp.float32)
    mean = jnp.mean(values, axis=-1, keepdims=True)
    centered = values - mean
    var = jnp.mean(centered * centered, axis=-1, keepdims=True)
    return centered * lax.rsqrt(var + 1e-05)


def project(block, weights):
    flat = block.reshape(-1, block.shape[-1])
    result = jnp.dot(flat, weights, preferred_element_type=jnp.float32)
    return result.reshape(block.shape[0], block.shape[1], weights.shape[1])


def gated(proj, first_flags, second_flags, hidden):
    both = first_flags[:, None, None] * second_flags[None, :, None]
    return (jax.nn.sigmoid(proj[..., :hidden]) * proj[..., hidden:] * both).astype(jnp.bfloat16)


def per_device(pair, mask, in_weights, gate_weight, out_weight):
    rows, cols, width = pair.shape
    hidden = out_weight.shape[0]
    row_at = lax.axis_index("row")
    col_at = lax.axis_index("col")
    flags = mask.astype(jnp.float32)
    row_flags = lax.dynamic_slice_in_dim(flags, row_at * rows, rows)
    col_flags = lax.dynamic_slice_in_dim(flags, col_at * cols, cols)
    normed = normalize(pair).astype(jnp.bfloat16)
    left_own = gated(project(normed, in_weights[:, : 2 * hidden]), row_flags, col_flags, hidden)
    left = lax.all_gather(left_own, "col", axis=0, tiled=False)
    right = gated(project(normed, in_weights[:, 2 * hidden :]), row_flags, col_flags, hidden)
    partial = jnp.einsum("nkic,kjc->nijc", left, right, preferred_element_type=jnp.float32)
    mixed = lax.psum_scatter(partial.astype(jnp.bfloat16), "row", scatter_dimension=0, tiled=False)
    mixed_normed = normalize(mixed).astype(jnp.bfloat16)
    gate = jax.nn.sigmoid(project(normed, gate_weight))
    value = project(mixed_normed, out_weight)
    return (gate * value).astype(jnp.bfloat16)


def solution(mesh):
    placed = (P(("parts", "row"), "col", None), P("parts"), P(), P(), P())
    return jax.shard_map(
        per_device,
        mesh=mesh,
        in_specs=placed,
        out_specs=P(("parts", "row"), "col", None),
        check_vma=False,
    )
```

time: 142 us -> 131 us (0.923)
  blocking collectives: 54.8 us -> 0 us
  waiting for transfers between devices: 21.4 us -> 69.3 us
  local copies, waits for them, and re-layouts: 29.3 us -> 23 us
    all_to_all x2 -> x0, blocking collectives: 54.8 us -> none  [the longest x1 42.5 us: per_device(): lax.all_to_all(lax.all_to_all(normed, 'col', split_axis=0, concat_axis=1,...]
    reduce_scatter x0 -> x1, waiting for transfers between devices: none -> 45.9 us  [per_device(): lax.psum_scatter(partial.astype(jnp.bfloat16), 'row', scatter_dimension=0...]
    reshape x3 -> x0, local copies, waits for them, and re-layouts: 25.8 us -> none  [the longest x1 12.9 us: per_device(): right_split = right.reshape(groups, parts, step, cols, hidden)]
    convert_element_type x1 -> x2, local copies, waits for them, and re-layouts: 2.36 us -> 13 us  [the longest x1 10.8 us: per_device(): partial.astype(jnp.bfloat16)]
    all_gather x0 -> x1, local copies, waits for them, and re-layouts: none -> 9.96 us  [per_device(): left = lax.all_gather(left_own, 'col', axis=0, tiled=False)]
    dot_general x4, matrix products: 3.49 us -> 6.06 us  [project(): result = jnp.dot(flat, weights, preferred_element_type=jnp.float32)]
    convert_element_type x2 -> x0, other arithmetic: 2.29 us -> none  [the longest x1 1.51 us: per_device(): mixed_normed = normalize(mixed).astype(jnp.bfloat16)]
    all_gather x2 -> x1, waiting for transfers between devices: 21.4 us -> 23.4 us  [per_device(): left = lax.all_gather(left_own, 'col', axis=0, tiled=False)]
  transfers between devices with their start and end apart: 2 -> 2, of which waited for: 2 -> 2; matrix products, arithmetic and copies ran while one was open for 12% -> 3% of each run, Pallas kernels for 0% -> 0%
where the time goes in v1:
time: 131 us; the launch traced here: 129 us
  waiting for transfers between devices  69.3 us (53%)
  local copies, waits for them, and re-layouts  23 us (18%)
  between operations  13.5 us (10%)
  matrix products  13.3 us (10%)
  other arithmetic  9.44 us (7%)
    reduce_scatter x1, waiting for transfers between devices, per_device(): lax.psum_scatter(partial.astype(jnp.bfloat16), 'row', scatter_dimension=0...  45.9 us
    all_gather x1, waiting for transfers between devices, per_device(): left = lax.all_gather(left_own, 'col', axis=0, tiled=False)  23.4 us
    convert_element_type x1, local copies, waits for them, and re-layouts, per_device(): partial.astype(jnp.bfloat16)  10.8 us
    all_gather x1, local copies, waits for them, and re-layouts, per_device(): left = lax.all_gather(left_own, 'col', axis=0, tiled=False)  9.96 us
    dot_general x1, matrix products, per_device(): jnp.einsum('nkic,kjc->nijc', left, right, preferred_element_type=jnp.floa...  7.22 us
    dot_general x4, matrix products, project(): result = jnp.dot(flat, weights, preferred_element_type=jnp.float32)  6.06 us
    reduce_sum x2, other arithmetic, normalize(): var = jnp.mean(centered * centered, axis=-1, keepdims=True)  3.52 us
    reduce_sum x2, other arithmetic, normalize(): mean = jnp.mean(values, axis=-1, keepdims=True)  3.02 us
  transfers between devices with their start and end apart: 2, of which 2 were waited for; matrix products, arithmetic and copies ran while one was open for 3% of the time, Pallas kernels for 0%

profile of v1, /device:TPU:17, one launch (start us, length us, event | category | flops | bytes accessed | tf_op | source)
XLA Modules:
  0.0 128.6 jit_solution(1358809510273289295)
XLA Ops:
  6.5 0.0 copy-start
  6.5 0.0 copy-start.1
  6.5 0.0 copy-start.3
  6.5 0.0 all-gather.3.cloned.1.call-start
  6.6 1.5 %convert_reduce_fusion.1 = f32[48,48]{1,0:T(8,128)S(1)} fusion(bf16[48,48,128]{2,1,0:T(8,128)(2,1)} %param.5), kind=kLoop, calls=%fused_computation.4 | loop fusion | flops 587520 | bytes 599040 | tf_op jit(solution)/shard_map/reduce_sum | solution.py:9
  8.1 1.8 %fusion.6 = f32[48,48]{1,0:T(8,128)S(1)} fusion(bf16[48,48,128]{2,1,0:T(8,128)(2,1)} %param.5, f32[48,48]{1,0:T(8,128)S(1)} %broadcast_multiply_fusion.2), kind=kLoop, calls=%fused_computation.13 | loop fusion | flops 1177344 | bytes 608256 | tf_op jit(solution)/shard_map/reduce_sum | solution.py:11
  9.9 0.0 copy-done.1
  9.9 0.0 copy-done.3
  9.9 0.8 fusion.27
  10.7 0.0 copy-start.5
  10.7 2.1 %fusion.29 = f32[48,48,256]{2,1,0:T(8,128)} fusion(bf16[48,48,128]{2,1,0:T(8,128)(2,1)S(1)} %copy-done.1, f32[48,48]{1,0:T(8,128)S(1)} %add_rsqrt_fusion.1, f32[48,48]{1,0:T(8,128)S(1)} %broadcast_multiply_fusion.2, bf16[128,512]{1,0:T(8,128)(2,1)S(1)} %copy-done.3), kind=kOutput, calls=%fused_computation.38 | convolution fusion | flops 152174592 | bytes 3063808 | tf_op jit(solution)/shard_map/dot_general | solution.py:17
  12.8 0.0 copy-done.5
  12.8 0.1 fusion.38
  12.8 0.1 broadcast_multiply_fusion
  12.9 2.8 %fusion.14 = (bf16[48,48,128]{2,1,0:T(8,128)(2,1)}, bf16[48,48,128,1]{2,1,0,3:T(8,128)(2,1)}) fusion(f32[48,48,256]{2,1,0:T(8,128)S(1)} %fusion.27, f32[48,48]{1,0:T(8,128)S(1)} %broadcast_multiply_fusion, f32[48,48,256]{2,1,0:T(8,128)} %fusion.29), kind=kLoop, calls=%fused_computation.22 | loop fusion | flops 3538944 | bytes 5907456 | tf_op jit(solution)/shard_map/convert_element_type | solution.py:23
  15.7 0.0 all-gather.3.cloned.1.call-update
  15.7 0.0 reduce-scatter.2.cloned.1.call-start
  15.8 2.2 %copy.14 = bf16[48,48,128,1]{0,1,3,2:T(8,128)(2,1)S(1)} copy(bf16[48,48,128,1]{2,1,0,3:T(8,128)(2,1)} %get-tuple-element.6) | data formatting | bytes 1179648 | tf_op jit(solution)/shard_map/convert_element_type | solution.py:23
  18.0 23.4 %all-gather.3.cloned.1.call-done = bf16[192,48,128]{2,1,0:T(8,128)(2,1)} async-done(((bf16[48,48,128]{2,1,0:T(8,128)(2,1)}), bf16[192,48,128]{2,1,0:T(8,128)(2,1)}) %all-gather.3.cloned.1.call-update) | async-done | bytes 2359312 | tf_op jit(solution)/shard_map/all_gather | solution.py:36
  41.4 10.0 %copy.11 = bf16[192,48,128]{1,0,2:T(8,128)(2,1)} copy(bf16[192,48,128]{2,1,0:T(8,128)(2,1)} %all-gather.3.cloned.1.call-done) | data formatting | bytes 4718592 | tf_op jit(solution)/shard_map/all_gather | solution.py:36
  51.4 7.2 %convert_bitcast_fusion = bf16[4,48,48,128]{1,2,0,3:T(8,128)(2,1)} fusion(bf16[48,48,128,1]{0,1,3,2:T(8,128)(2,1)S(1)} %copy.14, bf16[4,48,48,128]{2,1,0,3:T(8,128)(2,1)} %bitcast.32), kind=kOutput, calls=%fused_computation | convolution fusion | flops 114425856 | bytes 5308416 | tf_op jit(solution)/shard_map/nkic,kjc->nijc/dot_general | solution.py:38
  58.6 10.8 %copy.13 = bf16[4,48,48,128]{3,2,1,0:T(8,128)(2,1)} copy(bf16[4,48,48,128]{1,2,0,3:T(8,128)(2,1)} %convert_bitcast_fusion) | data formatting | bytes 4718592 | tf_op jit(solution)/shard_map/convert_element_type | solution.py:39
  69.4 0.0 reduce-scatter.2.cloned.1.call-update
  69.4 0.0 copy-done
  69.4 1.5 %fusion.4 = f32[48,48,128]{2,1,0:T(8,128)S(1)} fusion(bf16[48,48,128]{2,1,0:T(8,128)(2,1)S(1)} %copy-done.1, f32[48,48]{1,0:T(8,128)S(1)} %add_rsqrt_fusion.1, f32[48,48]{1,0:T(8,128)S(1)} %broadcast_multiply_fusion.2, bf16[128,128]{1,0:T(8,128)(2,1)S(1)} %copy-done), kind=kOutput, calls=%fused_computation.11 | convolution fusion | flops 77561856 | bytes 1820672 | tf_op jit(solution)/shard_map/dot_general | solution.py:17
  70.9 0.0 copy-start.4
  70.9 45.9 %reduce-scatter.2.cloned.1.call-done = bf16[1,48,48,128]{3,2,1,0:T(8,128)(2,1)} async-done(((bf16[4,48,48,128]{3,2,1,0:T(8,128)(2,1)}), bf16[1,48,48,128]{3,2,1,0:T(8,128)(2,1)}) %reduce-scatter.2.cloned.1.call-update) | async-done | bytes 589840 | tf_op jit(solution)/shard_map/reduce_scatter | solution.py:39
  116.8 0.0 copy-start.2
  116.8 1.5 %convert_reduce_fusion = f32[48,48]{1,0:T(8,128)S(1)} fusion(bf16[1,48,48,128]{3,2,1,0:T(8,128)(2,1)} %reduce-scatter.2.cloned.1.call-done), kind=kLoop, calls=%fused_computation.1 | loop fusion | flops 587520 | bytes 599040 | tf_op jit(solution)/shard_map/reduce_sum | solution.py:9
  118.3 1.8 %fusion.11 = f32[48,48]{1,0:T(8,128)S(1)} fusion(bf16[1,48,48,128]{3,2,1,0:T(8,128)(2,1)} %reduce-scatter.2.cloned.1.call-done, f32[48,48]{1,0:T(8,128)S(1)} %broadcast_multiply_fusion.1), kind=kLoop, calls=%fused_computation.18 | loop fusion | flops 1177344 | bytes 608256 | tf_op jit(solution)/shard_map/reduce_sum | solution.py:11
  120.1 0.0 copy-done.4
  120.1 0.0 copy-done.2
  120.1 1.7 %fusion.5 = bf16[48,48,128]{2,1,0:T(8,128)(2,1)} fusion(f32[48,48,128]{2,1,0:T(8,128)S(1)} %fusion.4, bf16[1,48,48,128]{3,2,1,0:T(8,128)(2,1)S(1)} %copy-done.2, f32[48,48]{1,0:T(8,128)S(1)} %add_rsqrt_fusion, f32[48,48]{1,0:T(8,128)S(1)} %broadcast_multiply_fusion.1, bf16[128,128]{1,0:T(8,128)(2,1)S(1)} %copy-done.4), kind=kOutput, calls=%fused_computation.12 | convolution fusion | flops 77266944 | bytes 2410496 | tf_op jit(solution)/shard_map/dot_general | solution.py:17
  (5 shorter events, 0.0 us)
Async XLA Ops:
  6.5 62.9 %copy-start = (bf16[128,128]{1,0:T(8,128)(2,1)S(1)}, bf16[128,128]{1,0:T(8,128)(2,1)}, u32[]{:S(2)}) copy-start(bf16[128,128]{1,0:T(8,128)(2,1)} %param.8) | copy-start | bytes 98308
  6.5 3.3 %copy-start.1 = (bf16[48,48,128]{2,1,0:T(8,128)(2,1)S(1)}, bf16[48,48,128]{2,1,0:T(8,128)(2,1)}, u32[]{:S(2)}) copy-start(bf16[48,48,128]{2,1,0:T(8,128)(2,1)} %param.5) | copy-start | bytes 1769476
  6.5 3.3 %copy-start.3 = (bf16[128,512]{1,0:T(8,128)(2,1)S(1)}, bf16[128,512]{1,0:T(8,128)(2,1)}, u32[]{:S(2)}) copy-start(bf16[128,512]{1,0:T(8,128)(2,1)} %param.7) | copy-start | bytes 393220
  6.5 34.9 %all-gather.3.cloned.1.call-start = ((), (), s32[]{:S(2)}) async-start(), calls=%async_computation.2 | async-start | bytes 2949120 | tf_op jit(solution)/shard_map/all_gather | solution.py:36
  10.7 2.1 %copy-start.5 = (s32[192]{0:T(256)S(1)}, s32[192]{0:T(256)}, u32[]{:S(2)}) copy-start(s32[192]{0:T(256)} %param.6) | copy-start | bytes 2308
  15.7 101.0 %reduce-scatter.2.cloned.1.call-start = ((), (), s32[]{:S(2)}) async-start(), calls=%async_computation.1 | async-start | bytes 2949120 | tf_op jit(solution)/shard_map/reduce_scatter | solution.py:39
  70.9 49.2 %copy-start.4 = (bf16[128,128]{1,0:T(8,128)(2,1)S(1)}, bf16[128,128]{1,0:T(8,128)(2,1)}, u32[]{:S(2)}) copy-start(bf16[128,128]{1,0:T(8,128)(2,1)} %param.9) | copy-start | bytes 98308
  116.8 3.3 %copy-start.2 = (bf16[1,48,48,128]{3,2,1,0:T(8,128)(2,1)S(1)}, bf16[1,48,48,128]{3,2,1,0:T(8,128)(2,1)}, u32[]{:S(2)}) copy-start(bf16[1,48,48,128]{3,2,1,0:T(8,128)(2,1)} %reduce-scatter.2.cloned.1.call-done) | copy-start | bytes 1769476
Sparse Core Ops, SparseCore 0:
  15.9 25.5 all-gather.2
  69.5 47.1 reduce-scatter.1

commit v2 on v1

v2 whole, which is shorter than its diff:
```python
import functools

import jax
import jax.numpy as jnp
from jax import lax
from jax.experimental import pallas as pl
from jax.experimental.pallas import tpu as pltpu
from jax.sharding import PartitionSpec as P

MESH = pl.DeviceIdType.MESH
SLAB = 4
GROUP = 4


def normalize(values):
    values = values.astype(jnp.float32)
    mean = jnp.mean(values, axis=-1, keepdims=True)
    centered = values - mean
    var = jnp.mean(centered * centered, axis=-1, keepdims=True)
    return centered * lax.rsqrt(var + 1e-05)


def kernel(n_row, n_col, chunks, pair, row_flags, col_flags, in_w, gate_w, out_w, out,
           normed, left_all, right, left32, total, sums, arrived,
           own_sem, fwd_sem, left_sem, out_sem, in_sem):
    rows, cols, width = pair.shape
    hidden = out_w.shape[0]
    piece = rows // chunks
    chips = n_col // 2
    z = lax.axis_index("row")
    col = lax.axis_index("col")
    chip = col // 2
    core = col % 2
    sibling = 2 * chip + 1 - core

    barrier = pltpu.get_barrier_semaphore()
    pl.semaphore_signal(barrier, inc=1, device_id={"col": sibling}, device_id_type=MESH)
    for d in range(1, chips):
        pl.semaphore_signal(
            barrier, inc=1, device_id={"col": 2 * ((chip + d) % chips) + core}, device_id_type=MESH
        )

    @pl.when(z > 0)
    def _():
        pl.semaphore_signal(barrier, inc=1, device_id={"row": z - 1}, device_id_type=MESH)

    @pl.when(z < n_row - 1)
    def _():
        pl.semaphore_signal(barrier, inc=1, device_id={"row": z + 1}, device_id_type=MESH)

    def gated(proj, k0):
        value = jax.nn.sigmoid(proj[:, :hidden]) * proj[:, hidden:]
        value = value.reshape(SLAB, cols, hidden)
        flags = row_flags[pl.ds(k0, SLAB), :][:, None, :] * col_flags[...][None, :, :]
        return (value * flags).astype(jnp.bfloat16)

    @pl.loop(0, rows // SLAB)
    def _(s):
        k0 = s * SLAB
        own = normalize(pair[pl.ds(k0, SLAB)]).astype(jnp.bfloat16)
        normed[pl.ds(k0, SLAB)] = own
        proj = jnp.dot(own.reshape(SLAB * cols, width), in_w[:, : 2 * hidden], preferred_element_type=jnp.float32)
        left_all[col, pl.ds(k0, SLAB)] = gated(proj, k0)

    pl.semaphore_wait(barrier, chips + (z > 0).astype(jnp.int32) + (z < n_row - 1).astype(jnp.int32))

    def own_copy(d):
        target = sibling if d == 0 else 2 * ((chip + d) % chips) + core
        return pltpu.make_async_remote_copy(
            src_ref=left_all.at[col], dst_ref=left_all.at[col],
            send_sem=own_sem.at[d], recv_sem=left_sem.at[col],
            device_id={"col": target}, device_id_type=MESH,
        )

    def fwd_copy(d):
        source = 2 * ((chip - d + chips) % chips) + core
        return pltpu.make_async_remote_copy(
            src_ref=left_all.at[source], dst_ref=left_all.at[source],
            send_sem=fwd_sem.at[d], recv_sem=left_sem.at[source],
            device_id={"col": sibling}, device_id_type=MESH,
        )

    def wait_left(source):
        pltpu.make_async_remote_copy(
            src_ref=left_all.at[source], dst_ref=left_all.at[source],
            send_sem=own_sem.at[0], recv_sem=left_sem.at[source],
            device_id={"col": sibling}, device_id_type=MESH,
        ).wait_recv()

    for d in range(1, chips):
        own_copy(d).start()
    own_copy(0).start()

    @pl.loop(0, rows // SLAB)
    def _(s):
        k0 = s * SLAB
        own = normed[pl.ds(k0, SLAB)]
        proj = jnp.dot(own.reshape(SLAB * cols, width), in_w[:, 2 * hidden :], preferred_element_type=jnp.float32)
        right[pl.ds(k0, SLAB)] = gated(proj, k0).astype(jnp.float32)

    def product(place, i0):
        def add(k, accs):
            other = right[k]
            return tuple(accs[g] + left32[k, pl.ds(i0 + g, 1), :] * other for g in range(GROUP))

        zero = jnp.zeros((cols, hidden), jnp.float32)
        accs = lax.fori_loop(0, rows, add, (zero,) * GROUP, unroll=4)
        for g in range(GROUP):
            total[place, i0 + g] = accs[g]

    def sum_copy(r, c, up):
        span = pl.ds(c * piece, piece)
        if up:
            slot, target = r, z + 1
        else:
            slot, target = jnp.where(r == z - 1, n_row, r), z - 1
        return pltpu.make_async_remote_copy(
            src_ref=sums.at[r, span], dst_ref=arrived.at[slot, span],
            send_sem=out_sem.at[r, c], recv_sem=in_sem.at[slot, c],
            device_id={"row": target}, device_id_type=MESH,
        )

    def wait_sum(slot, c):
        span = pl.ds(c * piece, piece)
        pltpu.make_async_remote_copy(
            src_ref=sums.at[0, span], dst_ref=arrived.at[slot, span],
            send_sem=out_sem.at[0, c], recv_sem=in_sem.at[slot, c],
            device_id={"row": z}, device_id_type=MESH,
        ).wait_recv()

    def one_target(r):
        @pl.loop(0, rows // SLAB)
        def _(s):
            left32[pl.ds(s * SLAB, SLAB)] = left_all[r, pl.ds(s * SLAB, SLAB)].astype(jnp.float32)

        @pl.when(r == z)
        def _():
            @pl.loop(0, rows // GROUP)
            def _(s):
                product(1, s * GROUP)

        @pl.when(r != z)
        def _():
            inner = jnp.logical_or(jnp.logical_and(r > z, z > 0), jnp.logical_and(r < z, z < n_row - 1))

            @pl.loop(0, chunks)
            def _(c):
                @pl.loop(0, piece // GROUP)
                def _(s):
                    product(0, c * piece + s * GROUP)

                span = pl.ds(c * piece, piece)

                @pl.when(inner)
                def _():
                    wait_sum(r, c)
                    sums[r, span] = (total[0, span] + arrived[r, span].astype(jnp.float32)).astype(jnp.bfloat16)

                @pl.when(jnp.logical_not(inner))
                def _():
                    sums[r, span] = total[0, span].astype(jnp.bfloat16)

                @pl.when(r > z)
                def _():
                    sum_copy(r, c, True).start()

                @pl.when(r < z)
                def _():
                    sum_copy(r, c, False).start()

    for d in range(chips):
        other_chip = (chip - d + chips) % chips
        if d > 0:
            wait_left(2 * other_chip + core)
            fwd_copy(d).start()
        wait_left(2 * other_chip + 1 - core)
        low = (2 * other_chip < chips).astype(jnp.int32)

        @pl.loop(0, 2)
        def _(j):
            one_target(2 * other_chip + low * j + (1 - low) * (1 - j))

    @pl.loop(0, chunks)
    def _(c):
        span = pl.ds(c * piece, piece)

        @pl.when(z > 0)
        def _():
            wait_sum(z, c)
            total[1, span] += arrived[z, span].astype(jnp.float32)

        @pl.when(z < n_row - 1)
        def _():
            wait_sum(n_row, c)
            total[1, span] += arrived[n_row, span].astype(jnp.float32)

        @pl.loop(0, piece // SLAB)
        def _(s):
            at = pl.ds(c * piece + s * SLAB, SLAB)
            mixed = normalize(total[1, at]).astype(jnp.bfloat16).reshape(SLAB * cols, hidden)
            value = jnp.dot(mixed, out_w[...], preferred_element_type=jnp.float32)
            gate = jnp.dot(normed[at].reshape(SLAB * cols, width), gate_w[...], preferred_element_type=jnp.float32)
            out[at] = (jax.nn.sigmoid(gate) * value).astype(jnp.bfloat16).reshape(SLAB, cols, width)

    for d in range(chips):
        own_copy(d).wait_send()
        if d > 0:
            fwd_copy(d).wait_send()

    @pl.loop(0, n_row)
    def _(r):
        @pl.when(r != z)
        def _():
            @pl.loop(0, chunks)
            def _(c):
                sum_copy(r, c, True).wait_send()


def per_device(pair, mask, in_weights, gate_weight, out_weight):
    rows, cols, width = pair.shape
    hidden = out_weight.shape[0]
    n_row = lax.axis_size("row")
    n_col = lax.axis_size("col")
    chunks = 4
    flags = mask.astype(jnp.float32)
    row_flags = lax.dynamic_slice_in_dim(flags, lax.axis_index("row") * rows, rows)
    col_flags = lax.dynamic_slice_in_dim(flags, lax.axis_index("col") * cols, cols)
    row_flags = jnp.broadcast_to(row_flags[:, None], (rows, hidden))
    col_flags = jnp.broadcast_to(col_flags[:, None], (cols, hidden))
    vmem = pl.BlockSpec(memory_space=pltpu.VMEM)
    return pl.pallas_call(
        functools.partial(kernel, n_row, n_col, chunks),
        out_shape=jax.ShapeDtypeStruct(pair.shape, jnp.bfloat16),
        in_specs=[vmem] * 6,
        out_specs=vmem,
        scratch_shapes=[
            pltpu.VMEM((rows, cols, width), jnp.bfloat16),
            pltpu.VMEM((n_col, rows, cols, hidden), jnp.bfloat16),
            pltpu.VMEM((rows, cols, hidden), jnp.float32),
            pltpu.VMEM((rows, cols, hidden), jnp.float32),
            pltpu.VMEM((2, rows, cols, hidden), jnp.float32),
            pltpu.VMEM((n_row, rows, cols, hidden), jnp.bfloat16),
            pltpu.VMEM((n_row + 1, rows, cols, hidden), jnp.bfloat16),
            pltpu.SemaphoreType.DMA((n_col // 2,)),
            pltpu.SemaphoreType.DMA((n_col // 2,)),
            pltpu.SemaphoreType.DMA((n_col,)),
            pltpu.SemaphoreType.DMA((n_row, chunks)),
            pltpu.SemaphoreType.DMA((n_row + 1, chunks)),
        ],
        compiler_params=pltpu.CompilerParams(
            collective_id=0, has_side_effects=True, vmem_limit_bytes=48 * 1024 * 1024
        ),
    )(pair, row_flags, col_flags, in_weights, gate_weight, out_weight)


def solution(mesh):
    placed = (P(("parts", "row"), "col", None), P("parts"), P(), P(), P())
    return jax.shard_map(
        per_device,
        mesh=mesh,
        in_specs=placed,
        out_specs=P(("parts", "row"), "col", None),
        check_vma=False,
    )
```

time: 131 us -> 67.5 us (0.52); the launches traced: 129 us -> 67.3 us
  waiting for transfers between devices: 69.3 us -> 0 us
  Pallas kernels: 0 us -> 63.5 us
  local copies, waits for them, and re-layouts: 23 us -> 3.68 us
  between operations: 13.5 us -> 0.03 us
  matrix products: 13.3 us -> 0 us
  other arithmetic: 9.44 us -> 0.01 us
    pallas_call x0 -> x1, Pallas kernels: none -> 63.5 us  [per_device(): pl.pallas_call(functools.partial(kernel, n_row, n_col, chunks), out_shape...]
    reduce_scatter x1 -> x0, waiting for transfers between devices: 45.9 us -> none  [per_device(): lax.psum_scatter(partial.astype(jnp.bfloat16), 'row', scatter_dimension=0...]
    all_gather x1 -> x0, waiting for transfers between devices: 23.4 us -> none  [per_device(): left = lax.all_gather(left_own, 'col', axis=0, tiled=False)]
    dot_general x5 -> x0, matrix products: 13.3 us -> none  [the longest x1 7.22 us: per_device(): jnp.einsum('nkic,kjc->nijc', left, right, preferred_element_type=jnp.floa...]
    convert_element_type x2 -> x0, local copies, waits for them, and re-layouts: 13 us -> none  [the longest x1 10.8 us: per_device(): partial.astype(jnp.bfloat16)]
    all_gather x1 -> x0, local copies, waits for them, and re-layouts: 9.96 us -> none  [per_device(): left = lax.all_gather(left_own, 'col', axis=0, tiled=False)]
    reduce_sum x4 -> x0, other arithmetic: 6.54 us -> none  [the longest x2 3.52 us: normalize(): var = jnp.mean(centered * centered, axis=-1, keepdims=True)]
    unnamed x12 -> x11, local copies, waits for them, and re-layouts: 0.03 us -> 3.46 us
  transfers between devices with their start and end apart: 2 -> 0, of which waited for: 2 -> 0; matrix products, arithmetic and copies ran while one was open for 3% -> 0% of each run, Pallas kernels for 0% -> 0%
where the time goes in v2:
time: 67.5 us; the launch traced here: 67.3 us
  Pallas kernels  63.5 us (94%)
  local copies, waits for them, and re-layouts  3.68 us (5%)
    pallas_call x1, Pallas kernels, per_device(): pl.pallas_call(functools.partial(kernel, n_row, n_col, chunks), out_shape...  63.5 us
    unnamed x11, local copies, waits for them, and re-layouts  3.46 us

profile of v2, /device:TPU:17, one launch (start us, length us, event | category | flops | bytes accessed | tf_op | source)
XLA Modules:
  0.0 67.3 jit_solution(911734550670764677)
XLA Ops:
  0.0 0.0 copy-start.4
  0.0 0.0 copy-start.3
  0.0 0.0 copy-start.2
  0.0 0.7 copy-done.4
  0.7 0.1 fusion
  0.8 0.1 broadcast_in_dim.5.col_flags
  0.8 0.1 broadcast_in_dim.4.row_flags
  0.9 0.0 copy-done.3
  0.9 0.0 copy-done.2
  0.9 0.0 copy-start
  0.9 1.1 %copy-done = bf16[48,48,128]{2,1,0:T(8,128)(2,1)S(1)} copy-done((bf16[48,48,128]{2,1,0:T(8,128)(2,1)S(1)}, bf16[48,48,128]{2,1,0:T(8,128)(2,1)}, u32[]{:S(2)}) %copy-start) | copy-done | bytes 589848
  2.0 0.0 copy-start.1
  2.0 0.9 %copy-done.1 = bf16[128,512]{1,0:T(8,128)(2,1)S(1)} copy-done((bf16[128,512]{1,0:T(8,128)(2,1)S(1)}, bf16[128,512]{1,0:T(8,128)(2,1)}, u32[]{:S(2)}) %copy-start.1) | copy-done | bytes 131096
  2.9 63.5 %shard_map.55 = bf16[48,48,128]{2,1,0:T(8,128)(2,1)S(1)} custom-call(bf16[48,48,128]{2,1,0:T(8,128)(2,1)S(1)} %copy-done, f32[48,128]{1,0:T(8,128)S(1)} %broadcast_in_dim.4.row_flags, f32[48,128]{1,0:T(8,128)S(1)} %broadcast_in_dim.5.col_flags, bf16[128,512]{1,0:T(8,128)(2,1)S(1)} %copy-done.1, bf16[128,128]{1,0:T(8,128)(2,1)S(1)} %copy-done.2, ...), custom_call_target="tpu_custom_call" | custom-call | tf_op jit(solution)/shard_map/pallas_call | solution.py:231
  66.4 0.8 %copy.7 = bf16[48,48,128]{2,1,0:T(8,128)(2,1)} copy(bf16[48,48,128]{2,1,0:T(8,128)(2,1)S(1)} %shard_map.55) | data formatting | bytes 1179648
  (1 shorter events, 0.0 us)
Async XLA Ops:
  0.0 0.7 %copy-start.4 = (s32[192]{0:T(256)S(1)}, s32[192]{0:T(256)}, u32[]{:S(2)}) copy-start(s32[192]{0:T(256)} %param.6) | copy-start | bytes 2308
  0.0 0.9 %copy-start.3 = (bf16[128,128]{1,0:T(8,128)(2,1)S(1)}, bf16[128,128]{1,0:T(8,128)(2,1)}, u32[]{:S(2)}) copy-start(bf16[128,128]{1,0:T(8,128)(2,1)} %out_w.1) | copy-start | bytes 98308
  0.0 0.9 %copy-start.2 = (bf16[128,128]{1,0:T(8,128)(2,1)S(1)}, bf16[128,128]{1,0:T(8,128)(2,1)}, u32[]{:S(2)}) copy-start(bf16[128,128]{1,0:T(8,128)(2,1)} %gate_w.1) | copy-start | bytes 98308
  0.9 1.1 %copy-start = (bf16[48,48,128]{2,1,0:T(8,128)(2,1)S(1)}, bf16[48,48,128]{2,1,0:T(8,128)(2,1)}, u32[]{:S(2)}) copy-start(bf16[48,48,128]{2,1,0:T(8,128)(2,1)} %pair.1) | copy-start | bytes 1769476
  2.0 0.9 %copy-start.1 = (bf16[128,512]{1,0:T(8,128)(2,1)S(1)}, bf16[128,512]{1,0:T(8,128)(2,1)}, u32[]{:S(2)}) copy-start(bf16[128,512]{1,0:T(8,128)(2,1)} %in_w.1) | copy-start | bytes 393220

commit v3 on v2

--- a/solution.py
+++ b/solution.py
@@ -9,6 +9,7 @@
 
 MESH = pl.DeviceIdType.MESH
 SLAB = 4
+FIRST = 16
 GROUP = 4
 
 
@@ -50,17 +51,17 @@
 
     def gated(proj, k0):
         value = jax.nn.sigmoid(proj[:, :hidden]) * proj[:, hidden:]
-        value = value.reshape(SLAB, cols, hidden)
-        flags = row_flags[pl.ds(k0, SLAB), :][:, None, :] * col_flags[...][None, :, :]
+        value = value.reshape(FIRST, cols, hidden)
+        flags = row_flags[pl.ds(k0, FIRST), :][:, None, :] * col_flags[...][None, :, :]
         return (value * flags).astype(jnp.bfloat16)
 
-    @pl.loop(0, rows // SLAB)
+    @pl.loop(0, rows // FIRST)
     def _(s):
-        k0 = s * SLAB
-        own = normalize(pair[pl.ds(k0, SLAB)]).astype(jnp.bfloat16)
-        normed[pl.ds(k0, SLAB)] = own
-        proj = jnp.dot(own.reshape(SLAB * cols, width), in_w[:, : 2 * hidden], preferred_element_type=jnp.float32)
-        left_all[col, pl.ds(k0, SLAB)] = gated(proj, k0)
+        k0 = s * FIRST
+        own = normalize(pair[pl.ds(k0, FIRST)]).astype(jnp.bfloat16)
+        normed[pl.ds(k0, FIRST)] = own
+        proj = jnp.dot(own.reshape(FIRST * cols, width), in_w[:, : 2 * hidden], preferred_element_type=jnp.float32)
+        left_all[col, pl.ds(k0, FIRST)] = gated(proj, k0)
 
     pl.semaphore_wait(barrier, chips + (z > 0).astype(jnp.int32) + (z < n_row - 1).astype(jnp.int32))
 
@@ -91,22 +92,20 @@
         own_copy(d).start()
     own_copy(0).start()
 
-    @pl.loop(0, rows // SLAB)
+    @pl.loop(0, rows // FIRST)
     def _(s):
-        k0 = s * SLAB
-        own = normed[pl.ds(k0, SLAB)]
-        proj = jnp.dot(own.reshape(SLAB * cols, width), in_w[:, 2 * hidden :], preferred_element_type=jnp.float32)
-        right[pl.ds(k0, SLAB)] = gated(proj, k0).astype(jnp.float32)
-
-    def product(place, i0):
+        k0 = s * FIRST
+        own = normed[pl.ds(k0, FIRST)]
+        proj = jnp.dot(own.reshape(FIRST * cols, width), in_w[:, 2 * hidden :], preferred_element_type=jnp.float32)
+        right[pl.ds(k0, FIRST)] = gated(proj, k0).astype(jnp.float32)
+
+    def product(i0):
         def add(k, accs):
             other = right[k]
             return tuple(accs[g] + left32[k, pl.ds(i0 + g, 1), :] * other for g in range(GROUP))
 
         zero = jnp.zeros((cols, hidden), jnp.float32)
-        accs = lax.fori_loop(0, rows, add, (zero,) * GROUP, unroll=4)
-        for g in range(GROUP):
-            total[place, i0 + g] = accs[g]
+        return lax.fori_loop(0, rows, add, (zero,) * GROUP, unroll=8)
 
     def sum_copy(r, c, up):
         span = pl.ds(c * piece, piece)
@@ -128,16 +127,39 @@
             device_id={"row": z}, device_id_type=MESH,
         ).wait_recv()
 
-    def one_target(r):
-        @pl.loop(0, rows // SLAB)
+    def finish(c):
+        span = pl.ds(c * piece, piece)
+
+        @pl.when(z > 0)
+        def _():
+            wait_sum(z, c)
+            total[span] += arrived[z, span].astype(jnp.float32)
+
+        @pl.when(z < n_row - 1)
+        def _():
+            wait_sum(n_row, c)
+            total[span] += arrived[n_row, span].astype(jnp.float32)
+
+        @pl.loop(0, piece // SLAB)
         def _(s):
-            left32[pl.ds(s * SLAB, SLAB)] = left_all[r, pl.ds(s * SLAB, SLAB)].astype(jnp.float32)
+            at = pl.ds(c * piece + s * SLAB, SLAB)
+            mixed = normalize(total[at]).astype(jnp.bfloat16).reshape(SLAB * cols, hidden)
+            value = jnp.dot(mixed, out_w[...], preferred_element_type=jnp.float32)
+            gate = jnp.dot(normed[at].reshape(SLAB * cols, width), gate_w[...], preferred_element_type=jnp.float32)
+            out[at] = (jax.nn.sigmoid(gate) * value).astype(jnp.bfloat16).reshape(SLAB, cols, width)
+
+    def one_target(r, closing):
+        @pl.loop(0, rows // FIRST)
+        def _(s):
+            left32[pl.ds(s * FIRST, FIRST)] = left_all[r, pl.ds(s * FIRST, FIRST)].astype(jnp.float32)
 
         @pl.when(r == z)
         def _():
             @pl.loop(0, rows // GROUP)
             def _(s):
-                product(1, s * GROUP)
+                accs = product(s * GROUP)
+                for g in range(GROUP):
+                    total[s * GROUP + g] = accs[g]
 
         @pl.when(r != z)
         def _():
@@ -145,20 +167,23 @@
 
             @pl.loop(0, chunks)
             def _(c):
-                @pl.loop(0, piece // GROUP)
-                def _(s):
-                    product(0, c * piece + s * GROUP)
-
-                span = pl.ds(c * piece, piece)
+                @pl.when(closing)
+                def _():
+                    finish(c)
+
+                accs = product(c * piece)
 
                 @pl.when(inner)
                 def _():
                     wait_sum(r, c)
-                    sums[r, span] = (total[0, span] + arrived[r, span].astype(jnp.float32)).astype(jnp.bfloat16)
+                    for g in range(GROUP):
+                        at = c * piece + g
+                        sums[r, at] = (accs[g] + arrived[r, at].astype(jnp.float32)).astype(jnp.bfloat16)
 
                 @pl.when(jnp.logical_not(inner))
                 def _():
-                    sums[r, span] = total[0, span].astype(jnp.bfloat16)
+                    for g in range(GROUP):
+                        sums[r, c * piece + g] = accs[g].astype(jnp.bfloat16)
 
                 @pl.when(r > z)
                 def _():
@@ -175,32 +200,21 @@
             fwd_copy(d).start()
         wait_left(2 * other_chip + 1 - core)
         low = (2 * other_chip < chips).astype(jnp.int32)
+        first = 2 * other_chip + 1 - low
+        last = 2 * other_chip + low
+        swap = (first == z).astype(jnp.int32)
 
         @pl.loop(0, 2)
         def _(j):
-            one_target(2 * other_chip + low * j + (1 - low) * (1 - j))
-
-    @pl.loop(0, chunks)
-    def _(c):
-        span = pl.ds(c * piece, piece)
-
-        @pl.when(z > 0)
-        def _():
-            wait_sum(z, c)
-            total[1, span] += arrived[z, span].astype(jnp.float32)
-
-        @pl.when(z < n_row - 1)
-        def _():
-            wait_sum(n_row, c)
-            total[1, span] += arrived[n_row, span].astype(jnp.float32)
-
-        @pl.loop(0, piece // SLAB)
-        def _(s):
-            at = pl.ds(c * piece + s * SLAB, SLAB)
-            mixed = normalize(total[1, at]).astype(jnp.bfloat16).reshape(SLAB * cols, hidden)
-            value = jnp.dot(mixed, out_w[...], preferred_element_type=jnp.float32)
-            gate = jnp.dot(normed[at].reshape(SLAB * cols, width), gate_w[...], preferred_element_type=jnp.float32)
-            out[at] = (jax.nn.sigmoid(gate) * value).astype(jnp.bfloat16).reshape(SLAB, cols, width)
+            at = (j + swap) % 2
+            target = at * last + (1 - at) * first
+            one_target(target, jnp.logical_and(jnp.logical_and(j == 1, d == chips - 1), jnp.logical_and(first != z, last != z)))
+
+    early = jnp.logical_and(last != z, first != z)
+
+    @pl.when(jnp.logical_not(early))
+    def _():
+        pl.loop(0, chunks)(finish)
 
     for d in range(chips):
         own_copy(d).wait_send()
@@ -221,7 +235,7 @@
     hidden = out_weight.shape[0]
     n_row = lax.axis_size("row")
     n_col = lax.axis_size("col")
-    chunks = 4
+    chunks = rows // GROUP
     flags = mask.astype(jnp.float32)
     row_flags = lax.dynamic_slice_in_dim(flags, lax.axis_index("row") * rows, rows)
     col_flags = lax.dynamic_slice_in_dim(flags, lax.axis_index("col") * cols, cols)
@@ -238,7 +252,7 @@
             pltpu.VMEM((n_col, rows, cols, hidden), jnp.bfloat16),
             pltpu.VMEM((rows, cols, hidden), jnp.float32),
             pltpu.VMEM((rows, cols, hidden), jnp.float32),
-            pltpu.VMEM((2, rows, cols, hidden), jnp.float32),
+            pltpu.VMEM((rows, cols, hidden), jnp.float32),
             pltpu.VMEM((n_row, rows, cols, hidden), jnp.bfloat16),
             pltpu.VMEM((n_row + 1, rows, cols, hidden), jnp.bfloat16),
             pltpu.SemaphoreType.DMA((n_col // 2,)),

time: 67.5 us -> 61.7 us (0.914)
  Pallas kernels: 63.5 us -> 57.7 us
    pallas_call x1, Pallas kernels: 63.5 us -> 57.7 us  [per_device(): pl.pallas_call(functools.partial(kernel, n_row, n_col, chunks), out_shape...]
where the time goes in v3:
time: 61.7 us; the launch traced here: 61.4 us
  Pallas kernels  57.7 us (94%)
  local copies, waits for them, and re-layouts  3.68 us (6%)
    pallas_call x1, Pallas kernels, per_device(): pl.pallas_call(functools.partial(kernel, n_row, n_col, chunks), out_shape...  57.7 us
    unnamed x11, local copies, waits for them, and re-layouts  3.46 us

profile of v3, /device:TPU:17, one launch (start us, length us, event | category | flops | bytes accessed | tf_op | source)
XLA Modules:
  0.0 61.4 jit_solution(1359842441979528695)
XLA Ops:
  0.0 0.0 copy-start.4
  0.0 0.0 copy-start.3
  0.0 0.0 copy-start.2
  0.0 0.7 %copy-done.4 = s32[192]{0:T(256)S(1)} copy-done((s32[192]{0:T(256)S(1)}, s32[192]{0:T(256)}, u32[]{:S(2)}) %copy-start.4) | copy-done | bytes 792
  0.7 0.1 fusion
  0.8 0.1 broadcast_in_dim.5.col_flags
  0.8 0.1 broadcast_in_dim.4.row_flags
  0.9 0.0 copy-done.3
  0.9 0.0 copy-done.2
  0.9 0.0 copy-start
  0.9 1.1 %copy-done = bf16[48,48,128]{2,1,0:T(8,128)(2,1)S(1)} copy-done((bf16[48,48,128]{2,1,0:T(8,128)(2,1)S(1)}, bf16[48,48,128]{2,1,0:T(8,128)(2,1)}, u32[]{:S(2)}) %copy-start) | copy-done | bytes 589848
  2.0 0.0 copy-start.1
  2.0 0.9 %copy-done.1 = bf16[128,512]{1,0:T(8,128)(2,1)S(1)} copy-done((bf16[128,512]{1,0:T(8,128)(2,1)S(1)}, bf16[128,512]{1,0:T(8,128)(2,1)}, u32[]{:S(2)}) %copy-start.1) | copy-done | bytes 131096
  2.9 57.7 %shard_map.55 = bf16[48,48,128]{2,1,0:T(8,128)(2,1)S(1)} custom-call(bf16[48,48,128]{2,1,0:T(8,128)(2,1)S(1)} %copy-done, f32[48,128]{1,0:T(8,128)S(1)} %broadcast_in_dim.4.row_flags, f32[48,128]{1,0:T(8,128)S(1)} %broadcast_in_dim.5.col_flags, bf16[128,512]{1,0:T(8,128)(2,1)S(1)} %copy-done.1, bf16[128,128]{1,0:T(8,128)(2,1)S(1)} %copy-done.2, ...), custom_call_target="tpu_custom_call" | custom-call | tf_op jit(solution)/shard_map/pallas_call | solution.py:245
  60.6 0.8 %copy.7 = bf16[48,48,128]{2,1,0:T(8,128)(2,1)} copy(bf16[48,48,128]{2,1,0:T(8,128)(2,1)S(1)} %shard_map.55) | data formatting | bytes 1179648
  (1 shorter events, 0.0 us)
Async XLA Ops:
  0.0 0.7 %copy-start.4 = (s32[192]{0:T(256)S(1)}, s32[192]{0:T(256)}, u32[]{:S(2)}) copy-start(s32[192]{0:T(256)} %param.6) | copy-start | bytes 2308
  0.0 0.9 %copy-start.3 = (bf16[128,128]{1,0:T(8,128)(2,1)S(1)}, bf16[128,128]{1,0:T(8,128)(2,1)}, u32[]{:S(2)}) copy-start(bf16[128,128]{1,0:T(8,128)(2,1)} %out_w.1) | copy-start | bytes 98308
  0.0 0.9 %copy-start.2 = (bf16[128,128]{1,0:T(8,128)(2,1)S(1)}, bf16[128,128]{1,0:T(8,128)(2,1)}, u32[]{:S(2)}) copy-start(bf16[128,128]{1,0:T(8,128)(2,1)} %gate_w.1) | copy-start | bytes 98308
  0.9 1.1 %copy-start = (bf16[48,48,128]{2,1,0:T(8,128)(2,1)S(1)}, bf16[48,48,128]{2,1,0:T(8,128)(2,1)}, u32[]{:S(2)}) copy-start(bf16[48,48,128]{2,1,0:T(8,128)(2,1)} %pair.1) | copy-start | bytes 1769476
  2.0 0.9 %copy-start.1 = (bf16[128,512]{1,0:T(8,128)(2,1)S(1)}, bf16[128,512]{1,0:T(8,128)(2,1)}, u32[]{:S(2)}) copy-start(bf16[128,512]{1,0:T(8,128)(2,1)} %in_w.1) | copy-start | bytes 393220

commit v4 on v3

--- a/solution.py
+++ b/solution.py
@@ -105,7 +105,7 @@
             return tuple(accs[g] + left32[k, pl.ds(i0 + g, 1), :] * other for g in range(GROUP))
 
         zero = jnp.zeros((cols, hidden), jnp.float32)
-        return lax.fori_loop(0, rows, add, (zero,) * GROUP, unroll=8)
+        return lax.fori_loop(0, rows, add, (zero,) * GROUP, unroll=16)
 
     def sum_copy(r, c, up):
         span = pl.ds(c * piece, piece)
@@ -227,7 +227,12 @@
         def _():
             @pl.loop(0, chunks)
             def _(c):
-                sum_copy(r, c, True).wait_send()
+                span = pl.ds(c * piece, piece)
+                pltpu.make_async_remote_copy(
+                    src_ref=sums.at[r, span], dst_ref=arrived.at[r, span],
+                    send_sem=out_sem.at[r, c], recv_sem=in_sem.at[r, c],
+                    device_id={"row": z}, device_id_type=MESH,
+                ).wait_send()
 
 
 def per_device(pair, mask, in_weights, gate_weight, out_weight):

time: 61.7 us -> 61.4 us (level)
  no operation moved by 1% of the time
where the time goes in v4:
time: 61.4 us; the launch traced here: 61.2 us
  Pallas kernels  57.5 us (94%)
  local copies, waits for them, and re-layouts  3.68 us (6%)
    pallas_call x1, Pallas kernels, per_device(): pl.pallas_call(functools.partial(kernel, n_row, n_col, chunks), out_shape...  57.5 us
    unnamed x11, local copies, waits for them, and re-layouts  3.46 us

profile of v4, /device:TPU:17, one launch (start us, length us, event | category | flops | bytes accessed | tf_op | source)
XLA Modules:
  0.0 61.2 jit_solution(11890673127745153860)
XLA Ops:
  0.0 0.0 copy-start.4
  0.0 0.0 copy-start.3
  0.0 0.0 copy-start.2
  0.0 0.7 %copy-done.4 = s32[192]{0:T(256)S(1)} copy-done((s32[192]{0:T(256)S(1)}, s32[192]{0:T(256)}, u32[]{:S(2)}) %copy-start.4) | copy-done | bytes 792
  0.7 0.1 fusion
  0.8 0.1 broadcast_in_dim.5.col_flags
  0.8 0.1 broadcast_in_dim.4.row_flags
  0.9 0.0 copy-done.3
  0.9 0.0 copy-done.2
  0.9 0.0 copy-start
  0.9 1.1 %copy-done = bf16[48,48,128]{2,1,0:T(8,128)(2,1)S(1)} copy-done((bf16[48,48,128]{2,1,0:T(8,128)(2,1)S(1)}, bf16[48,48,128]{2,1,0:T(8,128)(2,1)}, u32[]{:S(2)}) %copy-start) | copy-done | bytes 589848
  2.0 0.0 copy-start.1
  2.0 0.9 %copy-done.1 = bf16[128,512]{1,0:T(8,128)(2,1)S(1)} copy-done((bf16[128,512]{1,0:T(8,128)(2,1)S(1)}, bf16[128,512]{1,0:T(8,128)(2,1)}, u32[]{:S(2)}) %copy-start.1) | copy-done | bytes 131096
  2.9 57.5 %shard_map.55 = bf16[48,48,128]{2,1,0:T(8,128)(2,1)S(1)} custom-call(bf16[48,48,128]{2,1,0:T(8,128)(2,1)S(1)} %copy-done, f32[48,128]{1,0:T(8,128)S(1)} %broadcast_in_dim.4.row_flags, f32[48,128]{1,0:T(8,128)S(1)} %broadcast_in_dim.5.col_flags, bf16[128,512]{1,0:T(8,128)(2,1)S(1)} %copy-done.1, bf16[128,128]{1,0:T(8,128)(2,1)S(1)} %copy-done.2, ...), custom_call_target="tpu_custom_call" | custom-call | tf_op jit(solution)/shard_map/pallas_call | solution.py:250
  60.4 0.8 %copy.7 = bf16[48,48,128]{2,1,0:T(8,128)(2,1)} copy(bf16[48,48,128]{2,1,0:T(8,128)(2,1)S(1)} %shard_map.55) | data formatting | bytes 1179648
  (1 shorter events, 0.0 us)
Async XLA Ops:
  0.0 0.7 %copy-start.4 = (s32[192]{0:T(256)S(1)}, s32[192]{0:T(256)}, u32[]{:S(2)}) copy-start(s32[192]{0:T(256)} %param.6) | copy-start | bytes 2308
  0.0 0.9 %copy-start.3 = (bf16[128,128]{1,0:T(8,128)(2,1)S(1)}, bf16[128,128]{1,0:T(8,128)(2,1)}, u32[]{:S(2)}) copy-start(bf16[128,128]{1,0:T(8,128)(2,1)} %out_w.1) | copy-start | bytes 98308
  0.0 0.9 %copy-start.2 = (bf16[128,128]{1,0:T(8,128)(2,1)S(1)}, bf16[128,128]{1,0:T(8,128)(2,1)}, u32[]{:S(2)}) copy-start(bf16[128,128]{1,0:T(8,128)(2,1)} %gate_w.1) | copy-start | bytes 98308
  0.9 1.1 %copy-start = (bf16[48,48,128]{2,1,0:T(8,128)(2,1)S(1)}, bf16[48,48,128]{2,1,0:T(8,128)(2,1)}, u32[]{:S(2)}) copy-start(bf16[48,48,128]{2,1,0:T(8,128)(2,1)} %pair.1) | copy-start | bytes 1769476
  2.0 0.9 %copy-start.1 = (bf16[128,512]{1,0:T(8,128)(2,1)S(1)}, bf16[128,512]{1,0:T(8,128)(2,1)}, u32[]{:S(2)}) copy-start(bf16[128,512]{1,0:T(8,128)(2,1)} %in_w.1) | copy-start | bytes 393220

commit v5 on v4

--- a/solution.py
+++ b/solution.py
@@ -22,7 +22,7 @@
 
 
 def kernel(n_row, n_col, chunks, pair, row_flags, col_flags, in_w, gate_w, out_w, out,
-           normed, left_all, right, left32, total, sums, arrived,
+           gates, normed, left_all, right, left32, total, sums, arrived,
            own_sem, fwd_sem, left_sem, out_sem, in_sem):
     rows, cols, width = pair.shape
     hidden = out_w.shape[0]
@@ -145,8 +145,8 @@
             at = pl.ds(c * piece + s * SLAB, SLAB)
             mixed = normalize(total[at]).astype(jnp.bfloat16).reshape(SLAB * cols, hidden)
             value = jnp.dot(mixed, out_w[...], preferred_element_type=jnp.float32)
-            gate = jnp.dot(normed[at].reshape(SLAB * cols, width), gate_w[...], preferred_element_type=jnp.float32)
-            out[at] = (jax.nn.sigmoid(gate) * value).astype(jnp.bfloat16).reshape(SLAB, cols, width)
+            gate = gates[at].reshape(SLAB * cols, width)
+            out[at] = (gate * value).astype(jnp.bfloat16).reshape(SLAB, cols, width)
 
     def one_target(r, closing):
         @pl.loop(0, rows // FIRST)
@@ -195,6 +195,15 @@
 
     for d in range(chips):
         other_chip = (chip - d + chips) % chips
+        if d == chips - 1:
+
+            @pl.loop(0, rows // FIRST)
+            def _(s):
+                at = pl.ds(s * FIRST, FIRST)
+                flat = normed[at].reshape(FIRST * cols, width)
+                gate = jnp.dot(flat, gate_w[...], preferred_element_type=jnp.float32)
+                gates[at] = jax.nn.sigmoid(gate).reshape(FIRST, cols, width)
+
         if d > 0:
             wait_left(2 * other_chip + core)
             fwd_copy(d).start()
@@ -253,6 +262,7 @@
         in_specs=[vmem] * 6,
         out_specs=vmem,
         scratch_shapes=[
+            pltpu.VMEM((rows, cols, width), jnp.float32),
             pltpu.VMEM((rows, cols, width), jnp.bfloat16),
             pltpu.VMEM((n_col, rows, cols, hidden), jnp.bfloat16),
             pltpu.VMEM((rows, cols, hidden), jnp.float32),

time: 61.4 us -> 62 us (level)
  no operation moved by 1% of the time
where the time goes in v5:
time: 62 us; the launch traced here: 61.8 us
  Pallas kernels  58.1 us (94%)
  local copies, waits for them, and re-layouts  3.68 us (6%)
    pallas_call x1, Pallas kernels, per_device(): pl.pallas_call(functools.partial(kernel, n_row, n_col, chunks), out_shape...  58.1 us
    unnamed x11, local copies, waits for them, and re-layouts  3.46 us

profile of v5, /device:TPU:17, one launch (start us, length us, event | category | flops | bytes accessed | tf_op | source)
XLA Modules:
  0.0 61.8 jit_solution(5419850886482924408)
XLA Ops:
  0.0 0.0 copy-start.4
  0.0 0.0 copy-start.3
  0.0 0.0 copy-start.2
  0.0 0.7 %copy-done.4 = s32[192]{0:T(256)S(1)} copy-done((s32[192]{0:T(256)S(1)}, s32[192]{0:T(256)}, u32[]{:S(2)}) %copy-start.4) | copy-done | bytes 792
  0.7 0.1 fusion
  0.8 0.1 broadcast_in_dim.5.col_flags
  0.8 0.1 broadcast_in_dim.4.row_flags
  0.9 0.0 copy-done.3
  0.9 0.0 copy-done.2
  0.9 0.0 copy-start
  0.9 1.1 %copy-done = bf16[48,48,128]{2,1,0:T(8,128)(2,1)S(1)} copy-done((bf16[48,48,128]{2,1,0:T(8,128)(2,1)S(1)}, bf16[48,48,128]{2,1,0:T(8,128)(2,1)}, u32[]{:S(2)}) %copy-start) | copy-done | bytes 589848
  2.0 0.0 copy-start.1
  2.0 0.9 %copy-done.1 = bf16[128,512]{1,0:T(8,128)(2,1)S(1)} copy-done((bf16[128,512]{1,0:T(8,128)(2,1)S(1)}, bf16[128,512]{1,0:T(8,128)(2,1)}, u32[]{:S(2)}) %copy-start.1) | copy-done | bytes 131096
  2.9 58.1 %shard_map.55 = bf16[48,48,128]{2,1,0:T(8,128)(2,1)S(1)} custom-call(bf16[48,48,128]{2,1,0:T(8,128)(2,1)S(1)} %copy-done, f32[48,128]{1,0:T(8,128)S(1)} %broadcast_in_dim.4.row_flags, f32[48,128]{1,0:T(8,128)S(1)} %broadcast_in_dim.5.col_flags, bf16[128,512]{1,0:T(8,128)(2,1)S(1)} %copy-done.1, bf16[128,128]{1,0:T(8,128)(2,1)S(1)} %copy-done.2, ...), custom_call_target="tpu_custom_call" | custom-call | tf_op jit(solution)/shard_map/pallas_call | solution.py:259
  61.0 0.8 %copy.7 = bf16[48,48,128]{2,1,0:T(8,128)(2,1)} copy(bf16[48,48,128]{2,1,0:T(8,128)(2,1)S(1)} %shard_map.55) | data formatting | bytes 1179648
  (1 shorter events, 0.0 us)
Async XLA Ops:
  0.0 0.7 %copy-start.4 = (s32[192]{0:T(256)S(1)}, s32[192]{0:T(256)}, u32[]{:S(2)}) copy-start(s32[192]{0:T(256)} %param.6) | copy-start | bytes 2308
  0.0 0.9 %copy-start.3 = (bf16[128,128]{1,0:T(8,128)(2,1)S(1)}, bf16[128,128]{1,0:T(8,128)(2,1)}, u32[]{:S(2)}) copy-start(bf16[128,128]{1,0:T(8,128)(2,1)} %out_w.1) | copy-start | bytes 98308
  0.0 0.9 %copy-start.2 = (bf16[128,128]{1,0:T(8,128)(2,1)S(1)}, bf16[128,128]{1,0:T(8,128)(2,1)}, u32[]{:S(2)}) copy-start(bf16[128,128]{1,0:T(8,128)(2,1)} %gate_w.1) | copy-start | bytes 98308
  0.9 1.1 %copy-start = (bf16[48,48,128]{2,1,0:T(8,128)(2,1)S(1)}, bf16[48,48,128]{2,1,0:T(8,128)(2,1)}, u32[]{:S(2)}) copy-start(bf16[48,48,128]{2,1,0:T(8,128)(2,1)} %pair.1) | copy-start | bytes 1769476
  2.0 0.9 %copy-start.1 = (bf16[128,512]{1,0:T(8,128)(2,1)S(1)}, bf16[128,512]{1,0:T(8,128)(2,1)}, u32[]{:S(2)}) copy-start(bf16[128,512]{1,0:T(8,128)(2,1)} %in_w.1) | copy-start | bytes 393220
